TPU v7x, 32 devices: a whole 2x2x4 slice. The times are simulated.
32 devices in a mesh: groups: 2 (over y), patch: 4 (over z), head: 4 (over x, core).
Axes of the slice: x: 2, y: 2, z: 4, core: 2. Of those that a mesh axis runs over, the one named last changes fastest.
Arguments:
- queries: bfloat16 [1536, 1536], P(('groups', 'patch'), 'head'), parts along dimension 0, may hold values from -12.5 to 12.5
- fresh_keys: bfloat16 [1536, 1536], P(('groups', 'patch'), 'head'), parts along dimension 0, may hold values from -5 to 5
- fresh_values: bfloat16 [1536, 1536], P(('groups', 'patch'), 'head'), parts along dimension 0, may hold values from -6 to 6
- stale_keys: bfloat16 [1536, 1536], P(('groups', 'patch'), 'head'), parts along dimension 0, may hold values from -5 to 5
- stale_values: bfloat16 [1536, 1536], P(('groups', 'patch'), 'head'), parts along dimension 0, may hold values from -6 to 6
- out_weight: bfloat16 [1536, 5120], P('head', 'patch'), may hold values from -0.21875 to 0.21875
- gate_scale: float32 [10240], P(('groups', 'head')), parts along dimension 0, may hold values from 1 to 4
Outputs:
- branch_out: float32 [1536, 5120], P(('groups', 'patch'), 'head'), parts along dimension 0
There are 2 independent parts, one for each index of `groups`. A program takes and returns all parts, laid end to end along the dimension named above; an argument that names none is the same for every part. Nothing has to cross between parts.
All inputs are finite; a program needn't handle non-finite values.
Results may differ from a plain program's by a relative error of at most 0.006.
Values may be sent and summed in bfloat16 or wider, within the bound.
A program may use at most 64 MiB of HBM per device.

v0:
```python
import jax
import jax.numpy as jnp
from jax import lax
from jax.sharding import PartitionSpec as P

HEAD_DIM = 128


neg_large = -1e30


def head_view(matrix):
    return matrix.reshape(matrix.shape[0], -1, HEAD_DIM)


def block_scores(query_heads, key_block):
    return jnp.einsum(
        "qhd,khd->hqk", query_heads, head_view(key_block), preferred_element_type=jnp.float32
    ) * HEAD_DIM ** (-0.5)


def absorb(running, scores, value_block):
    run_max, run_total, run_acc = running
    new_max = jnp.maximum(run_max, jnp.max(scores, axis=2))
    factor = jnp.exp(run_max - new_max)
    weights = jnp.exp(scores - new_max[:, :, None])
    new_total = run_total * factor + jnp.sum(weights, axis=2)
    mixture = jnp.einsum(
        "hqk,khd->qhd",
        weights.astype(jnp.bfloat16),
        head_view(value_block),
        preferred_element_type=jnp.float32,
    )
    new_acc = run_acc * jnp.transpose(factor)[:, :, None] + mixture
    return (new_max, new_total, new_acc)


def empty_state(row_count, head_count):
    return (
        jnp.full((head_count, row_count), neg_large, jnp.float32),
        jnp.zeros((head_count, row_count), jnp.float32),
        jnp.zeros((row_count, head_count, HEAD_DIM), jnp.float32),
    )


def on_device(queries, fresh_keys, fresh_values, stale_keys, stale_values, out_weight, gate_scale):
    query_heads = head_view(queries)
    row_count = query_heads.shape[0]
    head_count = query_heads.shape[1]
    own_index = lax.axis_index("patch")
    own_start = own_index * row_count
    local = absorb(
        empty_state(row_count, head_count), block_scores(query_heads, fresh_keys), fresh_values
    )
    key_piece = lax.all_gather(stale_keys, "patch", axis=0, tiled=True)
    value_piece = lax.all_gather(stale_values, "patch", axis=0, tiled=True)
    key_count = key_piece.shape[0]
    key_step = 1024 if key_count > 1024 and key_count % 1024 == 0 else key_count

    def visit(block_index, inner):
        offset = block_index * key_step
        key_block = lax.dynamic_slice_in_dim(key_piece, offset, key_step, 0)
        value_block = lax.dynamic_slice_in_dim(value_piece, offset, key_step, 0)
        scores = block_scores(query_heads, key_block)
        position = offset + lax.iota(jnp.int32, key_step)
        own_rows = (position >= own_start) & (position < own_start + row_count)
        scores = jnp.where(own_rows[None, None, :], neg_large, scores)
        return absorb(inner, scores, value_block)

    run_max, run_total, run_acc = lax.fori_loop(0, key_count // key_step, visit, local)
    attended = (
        (run_acc / jnp.transpose(run_total)[:, :, None]).astype(jnp.bfloat16).reshape(row_count, -1)
    )
    partial_out = jnp.dot(
        attended,
        lax.all_gather(out_weight, "patch", axis=1, tiled=True),
        preferred_element_type=jnp.float32,
    )
    summed = lax.psum_scatter(partial_out, "head", scatter_dimension=1, tiled=True)
    return gate_scale[None, :] * summed


def solution(mesh):
    return jax.shard_map(
        on_device,
        mesh=mesh,
        in_specs=(
            P(("groups", "patch"), "head"),
            P(("groups", "patch"), "head"),
            P(("groups", "patch"), "head"),
            P(("groups", "patch"), "head"),
            P(("groups", "patch"), "head"),
            P("head", "patch"),
            P(("groups", "head")),
        ),
        out_specs=P(("groups", "patch"), "head"),
        check_vma=False,
    )
```

profile of v0, /device:TPU:25, one launch (start us, length us, event | category | flops | bytes accessed | tf_op | source)
XLA Modules:
  0.0 153.3 jit_solution(16892380855673942393)
XLA Ops:
  6.5 0.0 copy-start
  6.5 0.0 all-gather.2.cloned.1.call-start
  6.5 0.7 all-gather.2.cloned.1.call-update
  7.3 0.0 reduce-scatter.2.cloned.1.call-start
  7.3 0.0 copy-start.1
  7.3 14.9 %all_gather.9 = bf16[768,384]{1,0:T(8,128)(2,1)S(1)} all-gather(bf16[192,384]{1,0:T(8,128)(2,1)} %param.10), channel_id=1, replica_groups=mesh['groups'=2,'patch'=4,'head'=4] {'patch'}, dimensions={0}, use_global_device_ids=true | all-gather | bytes 737280 | tf_op jit(solution)/shard_map/all_gather | solution.py:55
  22.2 0.3 copy.27
  22.5 0.0 copy-done.2
  22.5 22.0 %all_gather.10 = bf16[768,384]{1,0:T(8,128)(2,1)S(1)} all-gather(bf16[192,384]{1,0:T(8,128)(2,1)S(1)} %copy-done.2), channel_id=1, replica_groups=mesh['groups'=2,'patch'=4,'head'=4] {'patch'}, dimensions={0}, use_global_device_ids=true | all-gather | bytes 737280 | tf_op jit(solution)/shard_map/all_gather | solution.py:56
  44.5 0.3 copy.30
  44.7 0.0 copy-done
  44.8 0.0 copy-done.1
  44.8 0.3 fusion.39
  45.0 0.5 fusion
  45.5 0.1 fusion.14
  45.7 0.5 fusion.1
  46.2 0.6 convolution_bitcast_fusion.1
  46.8 0.3 copy-done.4
  47.1 0.5 fusion.8
  47.6 47.6 %all-gather.2.cloned.1.call-done = bf16[384,5120]{1,0:T(8,128)(2,1)} async-done(((bf16[384,1280]{1,0:T(8,128)(2,1)}), bf16[384,5120]{1,0:T(8,128)(2,1)}) %all-gather.2.cloned.1.call-update) | async-done | bytes 3932176 | tf_op jit(solution)/shard_map/all_gather | solution.py:76
  95.2 5.2 %fusion.18 = f32[192,5120]{1,0:T(8,128)} fusion(bf16[384,5120]{1,0:T(8,128)(2,1)} %all-gather.2.cloned.1.call-done, bf16[3,24,8,128]{3,2,1,0:T(8,128)(2,1)S(1)} %fusion.8), kind=kOutput, calls=%fused_computation.23 | convolution fusion | flops 754974720 | bytes 8011776 | tf_op jit(solution)/shard_map/dot_general | solution.py:74
  100.4 0.0 reduce-scatter.2.cloned.1.call-update
  100.4 43.8 %reduce-scatter.2.cloned.1.call-done = f32[192,1280]{1,0:T(8,128)} async-done(((f32[192,5120]{1,0:T(8,128)}), f32[192,1280]{1,0:T(8,128)}) %reduce-scatter.2.cloned.1.call-update) | async-done | bytes 983056 | tf_op jit(solution)/shard_map/reduce_scatter | solution.py:79
  144.2 2.2 %broadcast_multiply_fusion = f32[192,1280]{1,0:T(8,128)} fusion(f32[192,1280]{1,0:T(8,128)} %reduce-scatter.2.cloned.1.call-done, f32[1280]{0:T(1024)S(1)} %copy-done.3), kind=kLoop, calls=%fused_computation.21 | loop fusion | flops 245760 | bytes 1971200 | tf_op jit(solution)/shard_map/mul | solution.py:80
  (7 shorter events, 0.0 us)
Async XLA Ops:
  6.5 38.2 %copy-start = (bf16[192,384]{1,0:T(8,128)(2,1)S(1)}, bf16[192,384]{1,0:T(8,128)(2,1)}, u32[]{:S(2)}) copy-start(bf16[192,384]{1,0:T(8,128)(2,1)} %param.7) | copy-start | bytes 442372
  6.5 15.9 %copy-start.2 = (bf16[192,384]{1,0:T(8,128)(2,1)S(1)}, bf16[192,384]{1,0:T(8,128)(2,1)}, u32[]{:S(2)}) copy-start(bf16[192,384]{1,0:T(8,128)(2,1)} %param.11) | copy-start | bytes 442372
  6.5 88.6 %all-gather.2.cloned.1.call-start = ((), (), s32[]{:S(2)}) async-start(), calls=%async_computation.1 | async-start | bytes 4915200 | tf_op jit(solution)/shard_map/all_gather | solution.py:76
  7.3 137.0 %reduce-scatter.2.cloned.1.call-start = ((), (), s32[]{:S(2)}) async-start(), calls=%async_computation.2 | async-start | bytes 4915200 | tf_op jit(solution)/shard_map/reduce_scatter | solution.py:79
  7.3 37.4 %copy-start.1 = (bf16[192,384]{1,0:T(8,128)(2,1)S(1)}, bf16[192,384]{1,0:T(8,128)(2,1)}, u32[]{:S(2)}) copy-start(bf16[192,384]{1,0:T(8,128)(2,1)} %param.8) | copy-start | bytes 442372
  46.2 0.9 copy-start.4
  100.4 43.9 %copy-start.3 = (f32[1280]{0:T(1024)S(1)}, f32[1280]{0:T(1024)}, u32[]{:S(2)}) copy-start(f32[1280]{0:T(1024)} %param.13) | copy-start | bytes 15364
Sparse Core Ops, SparseCore 0:
  8.9 86.2 all-gather.1
  100.5 43.6 reduce-scatter.1
where the time goes:
time: 155 us; the launch traced here: 153 us
  waiting for transfers between devices  92.2 us (59%)
  blocking collectives  36.9 us (24%)
  between operations  13.5 us (9%)
  matrix products  6.95 us (4%)
  other arithmetic  2.89 us (2%)
    all_gather x1, waiting for transfers between devices, on_device(): lax.all_gather(out_weight, 'patch', axis=1, tiled=True)  47.6 us
    reduce_scatter x1, waiting for transfers between devices, on_device(): lax.psum_scatter(partial_out, 'head', scatter_dimension=1, tiled=True)  43.8 us
    all_gather x1, blocking collectives, on_device(): value_piece = lax.all_gather(stale_values, 'patch', axis=0, tiled=True)  22 us
    all_gather x1, blocking collectives, on_device(): key_piece = lax.all_gather(stale_keys, 'patch', axis=0, tiled=True)  14.9 us
    dot_general x1, matrix products, on_device(): jnp.dot(attended, lax.all_gather(out_weight, 'patch', axis=1, tiled=True)...  5.17 us
  transfers between devices with their start and end apart: 2, of which 2 were waited for; matrix products, arithmetic and copies ran while one was open for 2% of the time, Pallas kernels for 0%

commit v1 on v0

--- a/solution.py
+++ b/solution.py
@@ -1,9 +1,15 @@
+import functools
+
 import jax
 import jax.numpy as jnp
 from jax import lax
+from jax.experimental import pallas as pl
+from jax.experimental.pallas import tpu as pltpu
 from jax.sharding import PartitionSpec as P
 
 HEAD_DIM = 128
+MESH = pl.DeviceIdType.MESH
+CORES = 2
 
 
 neg_large = -1e30
@@ -43,6 +49,289 @@
     )
 
 
+def sublayer_kernel(
+    n_patch, n_head, q_ref, fk_ref, fv_ref, sk_ref, sv_ref, w_ref, out_ref,
+    kbuf, vbuf, wsub, wbuf, abuf, ostage, obuf, top, total, acc,
+    kv_send, kv_recv, w_send, w_recv, z_send, x_send, sib_send, a_recv, o_send, o_recv,
+):
+    g, p, h = lax.axis_index("groups"), lax.axis_index("patch"), lax.axis_index("head")
+    core, chip = lax.rem(h, CORES), lax.div(h, CORES)
+    sibling = h + 1 - 2 * core
+    sub = wsub.shape[2]
+    heads = q_ref.shape[1] // HEAD_DIM
+    scale = HEAD_DIM ** (-0.5)
+
+    barrier = pltpu.get_barrier_semaphore()
+    for s in range(n_patch):
+        for j in range(n_head):
+            @pl.when(jnp.logical_or(p != s, h != j))
+            def _():
+                pl.semaphore_signal(barrier, inc=1, device_id=(g, s, j), device_id_type=MESH)
+    for j in range(n_head):
+        wsub[j] = w_ref[:, j * sub:(j + 1) * sub]
+    wbuf[h] = wsub[h]
+    pl.semaphore_wait(barrier, n_patch * n_head - 1)
+
+    def remote(src, dst, send, recv, patch, head):
+        return pltpu.make_async_remote_copy(
+            src_ref=src, dst_ref=dst, send_sem=send, recv_sem=recv,
+            device_id=(g, patch, head), device_id_type=MESH,
+        )
+
+    def neighbour(side):
+        return p + 1 - 2 * side
+
+    def has_neighbour(side):
+        return (p < n_patch - 1) if side == 0 else (p > 0)
+
+    def slab_at(side, d):
+        return p - d if side == 0 else p + d
+
+    def is_slab(side, d):
+        return (p - d >= 0) if side == 0 else jnp.logical_and(p + d < n_patch, d >= 1)
+
+    def kv_copy(side, which, s, src):
+        buf = (kbuf, vbuf)[which]
+        return remote(
+            src, buf.at[s], kv_send.at[side, which, s], kv_recv.at[which, s], neighbour(side), h
+        )
+
+    for which, src in ((0, sk_ref), (1, sv_ref)):
+        for side in range(2):
+            @pl.when(has_neighbour(side))
+            def _():
+                kv_copy(side, which, p, src).start()
+
+    def w_copy(j):
+        return remote(wsub.at[j], wbuf.at[h], w_send.at[j], w_recv.at[h], p, j)
+
+    for j in range(n_head):
+        @pl.when(h != j)
+        def _():
+            w_copy(j).start()
+
+    def absorb_block(keys, values, first):
+        for i in range(heads):
+            cols = slice(i * HEAD_DIM, (i + 1) * HEAD_DIM)
+            scores = lax.dot_general(
+                q_ref[:, cols], keys[:, cols], (((1,), (1,)), ((), ())),
+                preferred_element_type=jnp.float32,
+            )
+            new_top = jnp.max(scores, axis=1, keepdims=True)
+            if not first:
+                old_top = top[i]
+                new_top = jnp.maximum(old_top, new_top)
+                factor = jnp.exp((old_top - new_top) * scale)
+            weights = jnp.exp((scores - new_top) * scale)
+            new_total = jnp.sum(weights, axis=1, keepdims=True)
+            mixture = jnp.dot(
+                weights.astype(jnp.bfloat16), values[:, cols], preferred_element_type=jnp.float32
+            )
+            if not first:
+                new_total = new_total + total[i] * factor
+                mixture = mixture + acc[i] * factor
+            top[i] = new_top
+            total[i] = new_total
+            acc[i] = mixture
+
+    absorb_block(fk_ref[...], fv_ref[...], True)
+
+    def kv_step(d, carry):
+        for which in range(2):
+            for side in range(2):
+                s = slab_at(side, d)
+
+                @pl.when(is_slab(side, d))
+                def _():
+                    buf = (kbuf, vbuf)[which]
+                    copy = kv_copy(side, which, s, buf.at[s])
+                    copy.wait_recv()
+
+                    @pl.when(has_neighbour(side))
+                    def _():
+                        copy.start()
+        for side in range(2):
+            s = slab_at(side, d)
+
+            @pl.when(is_slab(side, d))
+            def _():
+                absorb_block(kbuf.at[s][...], vbuf.at[s][...], False)
+        return carry
+
+    lax.fori_loop(1, n_patch, kv_step, 0)
+
+    for i in range(heads):
+        abuf[p, h, :, i * HEAD_DIM:(i + 1) * HEAD_DIM] = (acc[i] / total[i]).astype(jnp.bfloat16)
+
+    def z_copy(side, s):
+        return remote(
+            abuf.at[s, h], abuf.at[s, h], z_send.at[side, s], a_recv.at[s, h], neighbour(side), h
+        )
+
+    def x_copy(xx, s):
+        return remote(
+            abuf.at[s, h], abuf.at[s, h], x_send.at[xx, s], a_recv.at[s, h], p, xx * CORES + core
+        )
+
+    def sib_copy(s, head):
+        return remote(
+            abuf.at[s, head], abuf.at[s, head], sib_send.at[s, head], a_recv.at[s, head], p, sibling
+        )
+
+    def spread(s):
+        for xx in range(n_head // CORES):
+            @pl.when(chip != xx)
+            def _():
+                x_copy(xx, s).start()
+        sib_copy(s, h).start()
+
+    for side in range(2):
+        @pl.when(has_neighbour(side))
+        def _():
+            z_copy(side, p).start()
+    spread(p)
+
+    for j in range(n_head):
+        @pl.when(h != j)
+        def _():
+            remote(wsub.at[j], wbuf.at[j], w_send.at[j], w_recv.at[j], p, j).wait_recv()
+
+    def o_copy(s):
+        return remote(ostage.at[s], obuf.at[h], o_send.at[s], o_recv.at[h], s, p)
+
+    def stays(s):
+        return jnp.logical_and(s == p, h == p)
+
+    def project(s):
+        for xx in range(n_head // CORES):
+            head = xx * CORES + 1 - core
+            sib_in = remote(
+                abuf.at[s, head], abuf.at[s, head], sib_send.at[s, h], a_recv.at[s, head], p, sibling
+            )
+            sib_in.wait_recv()
+        term = jnp.dot(abuf[s, 0], wbuf[0], preferred_element_type=jnp.float32)
+        for j in range(1, n_head):
+            term = term + jnp.dot(abuf[s, j], wbuf[j], preferred_element_type=jnp.float32)
+        ostage[s] = term.astype(jnp.bfloat16)
+
+        @pl.when(stays(s))
+        def _():
+            obuf[h] = ostage[s]
+
+        @pl.when(jnp.logical_not(stays(s)))
+        def _():
+            o_copy(s).start()
+
+    def spread_step(d, carry):
+        for side in range(2):
+            s = slab_at(side, d)
+
+            @pl.when(is_slab(side, d))
+            def _():
+                copy = z_copy(side, s)
+                copy.wait_recv()
+
+                @pl.when(has_neighbour(side))
+                def _():
+                    copy.start()
+                spread(s)
+        for side in range(2):
+            s = slab_at(side, d - 1)
+
+            @pl.when(is_slab(side, d - 1))
+            def _():
+                for xx in range(n_head // CORES):
+                    @pl.when(chip != xx)
+                    def _():
+                        head = xx * CORES + core
+                        remote(
+                            abuf.at[s, head], abuf.at[s, head], x_send.at[xx, s],
+                            a_recv.at[s, head], p, head,
+                        ).wait_recv()
+                        sib_copy(s, head).start()
+        for side in range(2):
+            s = slab_at(side, d - 1)
+
+            @pl.when(is_slab(side, d - 1))
+            def _():
+                project(s)
+        return carry
+
+    lax.fori_loop(1, n_patch + 1, spread_step, 0)
+
+    for j in range(n_head):
+        @pl.when(jnp.logical_or(p != h, h != j))
+        def _():
+            remote(ostage.at[0], obuf.at[j], o_send.at[0], o_recv.at[j], h, j).wait_recv()
+        out_ref[:, j * sub:(j + 1) * sub] = obuf[j]
+
+    for j in range(n_head):
+        @pl.when(h != j)
+        def _():
+            w_copy(j).wait_send()
+
+    def drain(s, carry):
+        for side in range(2):
+            passes = (s <= p) if side == 0 else (s >= p)
+
+            @pl.when(jnp.logical_and(passes, has_neighbour(side)))
+            def _():
+                kv_copy(side, 0, s, kbuf.at[s]).wait_send()
+                kv_copy(side, 1, s, vbuf.at[s]).wait_send()
+                z_copy(side, s).wait_send()
+        for xx in range(n_head // CORES):
+            @pl.when(chip != xx)
+            def _():
+                x_copy(xx, s).wait_send()
+            sib_copy(s, xx * CORES + core).wait_send()
+
+        @pl.when(jnp.logical_not(stays(s)))
+        def _():
+            o_copy(s).wait_send()
+        return carry
+
+    lax.fori_loop(0, n_patch, drain, 0)
+
+
+def fused_sublayer(n_patch, n_head, queries, fresh_keys, fresh_values, stale_keys, stale_values, out_weight):
+    rows, width = queries.shape
+    columns = out_weight.shape[1]
+    sub = columns // n_head
+    heads = width // HEAD_DIM
+    bf16, dma = jnp.bfloat16, pltpu.SemaphoreType.DMA
+    return pl.pallas_call(
+        functools.partial(sublayer_kernel, n_patch, n_head),
+        out_shape=jax.ShapeDtypeStruct((rows, columns), bf16),
+        in_specs=[pl.BlockSpec(memory_space=pltpu.VMEM)] * 6,
+        out_specs=pl.BlockSpec(memory_space=pltpu.VMEM),
+        scratch_shapes=[
+            pltpu.VMEM((n_patch, rows, width), bf16),
+            pltpu.VMEM((n_patch, rows, width), bf16),
+            pltpu.VMEM((n_head, width, sub), bf16),
+            pltpu.VMEM((n_head, width, sub), bf16),
+            pltpu.VMEM((n_patch, n_head, rows, width), bf16),
+            pltpu.VMEM((n_patch, rows, sub), bf16),
+            pltpu.VMEM((n_head, rows, sub), bf16),
+            pltpu.VMEM((heads, rows, 1), jnp.float32),
+            pltpu.VMEM((heads, rows, 1), jnp.float32),
+            pltpu.VMEM((heads, rows, HEAD_DIM), jnp.float32),
+            dma((2, 2, n_patch)),
+            dma((2, n_patch)),
+            dma((n_head,)),
+            dma((n_head,)),
+            dma((2, n_patch)),
+            dma((n_head // CORES, n_patch)),
+            dma((n_patch, n_head)),
+            dma((n_patch, n_head)),
+            dma((n_patch,)),
+            dma((n_head,)),
+        ],
+        compiler_params=pltpu.CompilerParams(
+            collective_id=0, has_side_effects=True, vmem_limit_bytes=40 * 1024 * 1024
+        ),
+    )(queries, fresh_keys, fresh_values, stale_keys, stale_values, out_weight)
+
+
 def on_device(queries, fresh_keys, fresh_values, stale_keys, stale_values, out_weight, gate_scale):
     query_heads = head_view(queries)
     row_count = query_heads.shape[0]
@@ -81,8 +370,16 @@
 
 
 def solution(mesh):
+    def fused(queries, fresh_keys, fresh_values, stale_keys, stale_values, out_weight, gate_scale):
+        summed = fused_sublayer(
+            n_patch, n_head, queries, fresh_keys, fresh_values, stale_keys, stale_values, out_weight
+        )
+        return gate_scale[None, :] * summed.astype(jnp.float32)
+
+    n_patch, n_head = mesh.shape["patch"], mesh.shape["head"]
+    square = n_patch == n_head and n_head % CORES == 0
     return jax.shard_map(
-        on_device,
+        fused if square else on_device,
         mesh=mesh,
         in_specs=(
             P(("groups", "patch"), "head"),

time: 155 us -> 65.5 us (0.42)
  waiting for transfers between devices: 92.2 us -> 0 us
  Pallas kernels: 0 us -> 58.4 us
  blocking collectives: 36.9 us -> 0 us
  between operations: 13.5 us -> 0.02 us
  matrix products: 6.95 us -> 0 us
  local copies, waits for them, and re-layouts: 0.84 us -> 5.75 us
  other arithmetic: 2.89 us -> 1.01 us
    pallas_call x0 -> x1, Pallas kernels: none -> 58.4 us  [fused_sublayer(): pl.pallas_call(functools.partial(sublayer_kernel, n_patch, n_head), out_s...]
    all_gather x1 -> x0, waiting for transfers between devices: 47.6 us -> none  [on_device(): lax.all_gather(out_weight, 'patch', axis=1, tiled=True)]
    reduce_scatter x1 -> x0, waiting for transfers between devices: 43.8 us -> none  [on_device(): lax.psum_scatter(partial_out, 'head', scatter_dimension=1, tiled=True)]
    all_gather x2 -> x0, blocking collectives: 36.9 us -> none  [the longest x1 22 us: on_device(): value_piece = lax.all_gather(stale_values, 'patch', axis=0, tiled=True)]
    dot_general x5 -> x0, matrix products: 6.95 us -> none  [the longest x1 5.17 us: on_device(): jnp.dot(attended, lax.all_gather(out_weight, 'patch', axis=1, tiled=True)...]
    unnamed x10 -> x14, local copies, waits for them, and re-layouts: 0.33 us -> 5.75 us
  transfers between devices with their start and end apart: 2 -> 0, of which waited for: 2 -> 0; matrix products, arithmetic and copies ran while one was open for 2% -> 0% of each run, Pallas kernels for 0% -> 0%
where the time goes in v1:
time: 65.5 us; the launch traced here: 65.2 us
  Pallas kernels  58.4 us (89%)
  local copies, waits for them, and re-layouts  5.75 us (9%)
  other arithmetic  1.01 us (2%)
    pallas_call x1, Pallas kernels, fused_sublayer(): pl.pallas_call(functools.partial(sublayer_kernel, n_patch, n_head), out_s...  58.4 us
    unnamed x14, local copies, waits for them, and re-layouts  5.75 us

profile of v1, /device:TPU:25, one launch (start us, length us, event | category | flops | bytes accessed | tf_op | source)
XLA Modules:
  0.0 65.2 jit_solution(14504169163576462998)
XLA Ops:
  0.0 0.0 copy-start
  0.0 1.2 %copy-done = bf16[384,1280]{1,0:T(8,128)(2,1)S(1)} copy-done((bf16[384,1280]{1,0:T(8,128)(2,1)S(1)}, bf16[384,1280]{1,0:T(8,128)(2,1)}, u32[]{:S(2)}) %copy-start) | copy-done | bytes 983064
  1.2 0.0 copy-start.1
  1.2 0.9 %copy-done.1 = bf16[192,384]{1,0:T(8,128)(2,1)S(1)} copy-done((bf16[192,384]{1,0:T(8,128)(2,1)S(1)}, bf16[192,384]{1,0:T(8,128)(2,1)}, u32[]{:S(2)}) %copy-start.1) | copy-done | bytes 147480
  2.1 0.0 copy-start.2
  2.1 0.9 %copy-done.2 = bf16[192,384]{1,0:T(8,128)(2,1)S(1)} copy-done((bf16[192,384]{1,0:T(8,128)(2,1)S(1)}, bf16[192,384]{1,0:T(8,128)(2,1)}, u32[]{:S(2)}) %copy-start.2) | copy-done | bytes 147480
  3.0 0.0 copy-start.3
  3.0 0.9 %copy-done.3 = bf16[192,384]{1,0:T(8,128)(2,1)S(1)} copy-done((bf16[192,384]{1,0:T(8,128)(2,1)S(1)}, bf16[192,384]{1,0:T(8,128)(2,1)}, u32[]{:S(2)}) %copy-start.3) | copy-done | bytes 147480
  3.9 0.0 copy-start.4
  3.9 0.9 %copy-done.4 = bf16[192,384]{1,0:T(8,128)(2,1)S(1)} copy-done((bf16[192,384]{1,0:T(8,128)(2,1)S(1)}, bf16[192,384]{1,0:T(8,128)(2,1)}, u32[]{:S(2)}) %copy-start.4) | copy-done | bytes 147480
  4.8 0.0 copy-start.5
  4.8 0.9 %copy-done.5 = bf16[192,384]{1,0:T(8,128)(2,1)S(1)} copy-done((bf16[192,384]{1,0:T(8,128)(2,1)S(1)}, bf16[192,384]{1,0:T(8,128)(2,1)}, u32[]{:S(2)}) %copy-start.5) | copy-done | bytes 147480
  5.8 0.0 copy-start.6
  5.8 58.4 %shard_map.73 = bf16[192,1280]{1,0:T(8,128)(2,1)S(1)} custom-call(bf16[192,384]{1,0:T(8,128)(2,1)S(1)} %copy-done.1, bf16[192,384]{1,0:T(8,128)(2,1)S(1)} %copy-done.2, bf16[192,384]{1,0:T(8,128)(2,1)S(1)} %copy-done.3, bf16[192,384]{1,0:T(8,128)(2,1)S(1)} %copy-done.4, bf16[192,384]{1,0:T(8,128)(2,1)S(1)} %copy-done.5, bf16[384,1280]{1,0:T(8,128)(2,1)S(1)} %copy-done), custom_call_target="tpu_custom_call" | custom-call | tf_op jit(solution)/shard_map/pallas_call | solution.py:302
  64.2 0.0 copy-done.6
  64.2 1.0 %convert_multiply_fusion = f32[192,1280]{1,0:T(8,128)} fusion(bf16[192,1280]{1,0:T(8,128)(2,1)S(1)} %shard_map.73, f32[1280]{0:T(1024)S(1)} %copy-done.6), kind=kLoop, calls=%fused_computation | loop fusion | flops 491520 | bytes 1479680 | tf_op jit(solution)/shard_map/mul | solution.py:377
Async XLA Ops:
  0.0 1.2 %copy-start = (bf16[384,1280]{1,0:T(8,128)(2,1)S(1)}, bf16[384,1280]{1,0:T(8,128)(2,1)}, u32[]{:S(2)}) copy-start(bf16[384,1280]{1,0:T(8,128)(2,1)} %w_ref.1) | copy-start | bytes 2949124
  1.2 0.9 %copy-start.1 = (bf16[192,384]{1,0:T(8,128)(2,1)S(1)}, bf16[192,384]{1,0:T(8,128)(2,1)}, u32[]{:S(2)}) copy-start(bf16[192,384]{1,0:T(8,128)(2,1)} %q_ref.1) | copy-start | bytes 442372
  2.1 0.9 %copy-start.2 = (bf16[192,384]{1,0:T(8,128)(2,1)S(1)}, bf16[192,384]{1,0:T(8,128)(2,1)}, u32[]{:S(2)}) copy-start(bf16[192,384]{1,0:T(8,128)(2,1)} %fk_ref.1) | copy-start | bytes 442372
  3.0 0.9 %copy-start.3 = (bf16[192,384]{1,0:T(8,128)(2,1)S(1)}, bf16[192,384]{1,0:T(8,128)(2,1)}, u32[]{:S(2)}) copy-start(bf16[192,384]{1,0:T(8,128)(2,1)} %fv_ref.1) | copy-start | bytes 442372
  3.9 0.9 %copy-start.4 = (bf16[192,384]{1,0:T(8,128)(2,1)S(1)}, bf16[192,384]{1,0:T(8,128)(2,1)}, u32[]{:S(2)}) copy-start(bf16[192,384]{1,0:T(8,128)(2,1)} %sk_ref.1) | copy-start | bytes 442372
  4.8 0.9 %copy-start.5 = (bf16[192,384]{1,0:T(8,128)(2,1)S(1)}, bf16[192,384]{1,0:T(8,128)(2,1)}, u32[]{:S(2)}) copy-start(bf16[192,384]{1,0:T(8,128)(2,1)} %sv_ref.1) | copy-start | bytes 442372
  5.8 58.4 %copy-start.6 = (f32[1280]{0:T(1024)S(1)}, f32[1280]{0:T(1024)}, u32[]{:S(2)}) copy-start(f32[1280]{0:T(1024)} %param.13) | copy-start | bytes 15364

commit v2 on v1

v2 whole, which is shorter than its diff:
```python
import functools

import jax
import jax.numpy as jnp
from jax import lax
from jax.experimental import pallas as pl
from jax.experimental.pallas import tpu as pltpu
from jax.sharding import PartitionSpec as P

HEAD_DIM = 128
MESH = pl.DeviceIdType.MESH
CORES = 2


neg_large = -1e30


def head_view(matrix):
    return matrix.reshape(matrix.shape[0], -1, HEAD_DIM)


def block_scores(query_heads, key_block):
    return jnp.einsum(
        "qhd,khd->hqk", query_heads, head_view(key_block), preferred_element_type=jnp.float32
    ) * HEAD_DIM ** (-0.5)


def absorb(running, scores, value_block):
    run_max, run_total, run_acc = running
    new_max = jnp.maximum(run_max, jnp.max(scores, axis=2))
    factor = jnp.exp(run_max - new_max)
    weights = jnp.exp(scores - new_max[:, :, None])
    new_total = run_total * factor + jnp.sum(weights, axis=2)
    mixture = jnp.einsum(
        "hqk,khd->qhd",
        weights.astype(jnp.bfloat16),
        head_view(value_block),
        preferred_element_type=jnp.float32,
    )
    new_acc = run_acc * jnp.transpose(factor)[:, :, None] + mixture
    return (new_max, new_total, new_acc)


def empty_state(row_count, head_count):
    return (
        jnp.full((head_count, row_count), neg_large, jnp.float32),
        jnp.zeros((head_count, row_count), jnp.float32),
        jnp.zeros((row_count, head_count, HEAD_DIM), jnp.float32),
    )


def sublayer_kernel(
    n_patch, n_head, q_hbm, fk_hbm, fv_hbm, sk_hbm, sv_hbm, w_hbm, out_ref,
    q_ref, fk_ref, fv_ref, w_ref,
    kbuf, vbuf, wsub, wbuf, abuf, ostage, obuf, top, total, acc,
    load, kv_send, kv_recv, w_send, w_recv, z_send, x_send, sib_send, a_recv, o_send, o_recv,
):
    g, p, h = lax.axis_index("groups"), lax.axis_index("patch"), lax.axis_index("head")
    core, chip = lax.rem(h, CORES), lax.div(h, CORES)
    sibling = h + 1 - 2 * core
    sub = wsub.shape[2]
    heads = q_ref.shape[1] // HEAD_DIM
    chips = n_head // CORES
    scale = HEAD_DIM ** (-0.5)

    def columns(i):
        return pl.ds(pl.multiple_of(i * HEAD_DIM, HEAD_DIM), HEAD_DIM)

    barrier = pltpu.get_barrier_semaphore()
    for s in range(n_patch):
        for j in range(n_head):
            @pl.when(jnp.logical_or(p != s, h != j))
            def _():
                pl.semaphore_signal(barrier, inc=1, device_id=(g, s, j), device_id_type=MESH)
    loads = [
        pltpu.make_async_copy(src, dst, load.at[k])
        for k, (src, dst) in enumerate(
            ((w_hbm, w_ref), (q_hbm, q_ref), (fk_hbm, fk_ref), (fv_hbm, fv_ref))
        )
    ]
    for copy in loads:
        copy.start()
    pl.semaphore_wait(barrier, n_patch * n_head - 1)

    def remote(src, dst, send, recv, patch, head):
        return pltpu.make_async_remote_copy(
            src_ref=src, dst_ref=dst, send_sem=send, recv_sem=recv,
            device_id=(g, patch, head), device_id_type=MESH,
        )

    def neighbour(side):
        return p + 1 - 2 * side

    def has_neighbour(side):
        return (p < n_patch - 1) if side == 0 else (p > 0)

    def slab_at(side, d):
        return p - d if side == 0 else p + d

    def is_slab(side, d):
        return (p - d >= 0) if side == 0 else jnp.logical_and(p + d < n_patch, d >= 1)

    def kv_copy(side, which, s, i, src):
        buf = (kbuf, vbuf)[which]
        return remote(
            src.at[:, columns(i)], buf.at[s, :, columns(i)], kv_send.at[side, which, s, i],
            kv_recv.at[which, s, i], neighbour(side), h,
        )

    def send_own(i):
        for which, src in ((0, sk_hbm), (1, sv_hbm)):
            for side in range(2):
                @pl.when(has_neighbour(side))
                def _():
                    kv_copy(side, which, p, i, src).start()

    send_own(0)

    def w_copy(j):
        return remote(wsub.at[j], wbuf.at[h], w_send.at[j], w_recv.at[h], p, j)

    loads[0].wait()
    for j in range(n_head):
        wsub[j] = w_ref[:, j * sub:(j + 1) * sub]

        @pl.when(h != j)
        def _():
            w_copy(j).start()
    wbuf[h] = wsub[h]
    for copy in loads[1:]:
        copy.wait()

    def absorb_block(i, keys, values, first):
        scores = lax.dot_general(
            q_ref[:, columns(i)], keys, (((1,), (1,)), ((), ())),
            preferred_element_type=jnp.float32,
        )
        new_top = jnp.max(scores, axis=1, keepdims=True)
        if not first:
            old_top = top[...]
            new_top = jnp.maximum(old_top, new_top)
            factor = jnp.exp((old_top - new_top) * scale)
        weights = jnp.exp((scores - new_top) * scale)
        new_total = jnp.sum(weights, axis=1, keepdims=True)
        mixture = jnp.dot(weights.astype(jnp.bfloat16), values, preferred_element_type=jnp.float32)
        if not first:
            new_total = new_total + total[...] * factor
            mixture = mixture + acc[...] * factor
        top[...] = new_top
        total[...] = new_total
        acc[...] = mixture

    def kv_step(i, d):
        for which in range(2):
            for side in range(2):
                s = slab_at(side, d)

                @pl.when(is_slab(side, d))
                def _():
                    copy = kv_copy(side, which, s, i, (kbuf, vbuf)[which].at[s])
                    copy.wait_recv()

                    @pl.when(has_neighbour(side))
                    def _():
                        copy.start()

        @pl.when(jnp.logical_and(d == 1, i + 1 < heads))
        def _():
            send_own(i + 1)
        for side in range(2):
            s = slab_at(side, d)

            @pl.when(is_slab(side, d))
            def _():
                absorb_block(i, kbuf[s, :, columns(i)], vbuf[s, :, columns(i)], False)

    def piece(s, head, i):
        return abuf.at[s, head, :, columns(i)]

    def z_copy(side, s, i):
        return remote(
            piece(s, h, i), piece(s, h, i), z_send.at[side, s, i], a_recv.at[s, h, i],
            neighbour(side), h,
        )

    def x_copy(xx, s, i):
        return remote(
            piece(s, h, i), piece(s, h, i), x_send.at[xx, s, i], a_recv.at[s, h, i],
            p, xx * CORES + core,
        )

    def sib_copy(s, head, i):
        return remote(
            piece(s, head, i), piece(s, head, i), sib_send.at[s, head, i], a_recv.at[s, head, i],
            p, sibling,
        )

    def spread(s, i):
        for xx in range(chips):
            @pl.when(chip != xx)
            def _():
                x_copy(xx, s, i).start()
        sib_copy(s, h, i).start()

    def o_copy(s):
        return remote(ostage.at[s], obuf.at[h], o_send.at[s], o_recv.at[h], s, p)

    def stays(s):
        return jnp.logical_and(s == p, h == p)

    def project(s):
        for i in range(heads):
            for xx in range(chips):
                head = xx * CORES + 1 - core
                remote(
                    piece(s, head, i), piece(s, head, i), sib_send.at[s, h, i],
                    a_recv.at[s, head, i], p, sibling,
                ).wait_recv()
        term = jnp.dot(abuf[s, 0], wbuf[0], preferred_element_type=jnp.float32)
        for j in range(1, n_head):
            term = term + jnp.dot(abuf[s, j], wbuf[j], preferred_element_type=jnp.float32)
        ostage[s] = term.astype(jnp.bfloat16)

        @pl.when(stays(s))
        def _():
            obuf[h] = ostage[s]

        @pl.when(jnp.logical_not(stays(s)))
        def _():
            o_copy(s).start()

    def spread_step(i, d):
        for side in range(2):
            s = slab_at(side, d)

            @pl.when(is_slab(side, d))
            def _():
                copy = z_copy(side, s, i)
                copy.wait_recv()

                @pl.when(has_neighbour(side))
                def _():
                    copy.start()
                spread(s, i)
        for side in range(2):
            s = slab_at(side, d - 1)

            @pl.when(is_slab(side, d - 1))
            def _():
                for xx in range(chips):
                    @pl.when(chip != xx)
                    def _():
                        head = xx * CORES + core
                        remote(
                            piece(s, head, i), piece(s, head, i), x_send.at[xx, s, i],
                            a_recv.at[s, head, i], p, head,
                        ).wait_recv()
                        sib_copy(s, head, i).start()

    def head_step(i, carry):
        @pl.when(i < heads)
        def _():
            absorb_block(i, fk_ref[:, columns(i)], fv_ref[:, columns(i)], True)

        @pl.when(i == heads)
        def _():
            for j in range(n_head):
                @pl.when(h != j)
                def _():
                    remote(wsub.at[j], wbuf.at[j], w_send.at[j], w_recv.at[j], p, j).wait_recv()

        def hop(d, inner):
            @pl.when(jnp.logical_and(i < heads, d < n_patch))
            def _():
                kv_step(i, d)

            @pl.when(i >= 1)
            def _():
                spread_step(i - 1, d)

            @pl.when(i == heads)
            def _():
                for side in range(2):
                    @pl.when(is_slab(side, d - 1))
                    def _():
                        project(slab_at(side, d - 1))
            return inner

        lax.fori_loop(1, n_patch + 1, hop, 0)

        @pl.when(i < heads)
        def _():
            abuf[p, h, :, columns(i)] = (acc[...] / total[...]).astype(jnp.bfloat16)
            for side in range(2):
                @pl.when(has_neighbour(side))
                def _():
                    z_copy(side, p, i).start()
            spread(p, i)
        return carry

    lax.fori_loop(0, heads + 1, head_step, 0)

    for j in range(n_head):
        @pl.when(jnp.logical_or(p != h, h != j))
        def _():
            remote(ostage.at[0], obuf.at[j], o_send.at[0], o_recv.at[j], h, j).wait_recv()
        out_ref[:, j * sub:(j + 1) * sub] = obuf[j]

    for j in range(n_head):
        @pl.when(h != j)
        def _():
            w_copy(j).wait_send()

    def drain(s, carry):
        def drain_head(i, inner):
            for side in range(2):
                passes = (s <= p) if side == 0 else (s >= p)

                @pl.when(jnp.logical_and(passes, has_neighbour(side)))
                def _():
                    kv_copy(side, 0, s, i, kbuf.at[s]).wait_send()
                    kv_copy(side, 1, s, i, vbuf.at[s]).wait_send()
                    z_copy(side, s, i).wait_send()
            for xx in range(chips):
                @pl.when(chip != xx)
                def _():
                    x_copy(xx, s, i).wait_send()
                sib_copy(s, xx * CORES + core, i).wait_send()
            return inner

        lax.fori_loop(0, heads, drain_head, 0)

        @pl.when(jnp.logical_not(stays(s)))
        def _():
            o_copy(s).wait_send()
        return carry

    lax.fori_loop(0, n_patch, drain, 0)


def fused_sublayer(n_patch, n_head, queries, fresh_keys, fresh_values, stale_keys, stale_values, out_weight):
    rows, width = queries.shape
    columns = out_weight.shape[1]
    sub = columns // n_head
    heads = width // HEAD_DIM
    bf16, dma = jnp.bfloat16, pltpu.SemaphoreType.DMA
    return pl.pallas_call(
        functools.partial(sublayer_kernel, n_patch, n_head),
        out_shape=jax.ShapeDtypeStruct((rows, columns), bf16),
        in_specs=[pl.BlockSpec(memory_space=pl.ANY)] * 6,
        out_specs=pl.BlockSpec(memory_space=pltpu.VMEM),
        scratch_shapes=[
            pltpu.VMEM((rows, width), bf16),
            pltpu.VMEM((rows, width), bf16),
            pltpu.VMEM((rows, width), bf16),
            pltpu.VMEM((width, columns), bf16),
            pltpu.VMEM((n_patch, rows, width), bf16),
            pltpu.VMEM((n_patch, rows, width), bf16),
            pltpu.VMEM((n_head, width, sub), bf16),
            pltpu.VMEM((n_head, width, sub), bf16),
            pltpu.VMEM((n_patch, n_head, rows, width), bf16),
            pltpu.VMEM((n_patch, rows, sub), bf16),
            pltpu.VMEM((n_head, rows, sub), bf16),
            pltpu.VMEM((rows, 1), jnp.float32),
            pltpu.VMEM((rows, 1), jnp.float32),
            pltpu.VMEM((rows, HEAD_DIM), jnp.float32),
            dma((4,)),
            dma((2, 2, n_patch, heads)),
            dma((2, n_patch, heads)),
            dma((n_head,)),
            dma((n_head,)),
            dma((2, n_patch, heads)),
            dma((n_head // CORES, n_patch, heads)),
            dma((n_patch, n_head, heads)),
            dma((n_patch, n_head, heads)),
            dma((n_patch,)),
            dma((n_head,)),
        ],
        compiler_params=pltpu.CompilerParams(
            collective_id=0, has_side_effects=True, vmem_limit_bytes=56 * 1024 * 1024
        ),
    )(queries, fresh_keys, fresh_values, stale_keys, stale_values, out_weight)


def on_device(queries, fresh_keys, fresh_values, stale_keys, stale_values, out_weight, gate_scale):
    query_heads = head_view(queries)
    row_count = query_heads.shape[0]
    head_count = query_heads.shape[1]
    own_index = lax.axis_index("patch")
    own_start = own_index * row_count
    local = absorb(
        empty_state(row_count, head_count), block_scores(query_heads, fresh_keys), fresh_values
    )
    key_piece = lax.all_gather(stale_keys, "patch", axis=0, tiled=True)
    value_piece = lax.all_gather(stale_values, "patch", axis=0, tiled=True)
    key_count = key_piece.shape[0]
    key_step = 1024 if key_count > 1024 and key_count % 1024 == 0 else key_count

    def visit(block_index, inner):
        offset = block_index * key_step
        key_block = lax.dynamic_slice_in_dim(key_piece, offset, key_step, 0)
        value_block = lax.dynamic_slice_in_dim(value_piece, offset, key_step, 0)
        scores = block_scores(query_heads, key_block)
        position = offset + lax.iota(jnp.int32, key_step)
        own_rows = (position >= own_start) & (position < own_start + row_count)
        scores = jnp.where(own_rows[None, None, :], neg_large, scores)
        return absorb(inner, scores, value_block)

    run_max, run_total, run_acc = lax.fori_loop(0, key_count // key_step, visit, local)
    attended = (
        (run_acc / jnp.transpose(run_total)[:, :, None]).astype(jnp.bfloat16).reshape(row_count, -1)
    )
    partial_out = jnp.dot(
        attended,
        lax.all_gather(out_weight, "patch", axis=1, tiled=True),
        preferred_element_type=jnp.float32,
    )
    summed = lax.psum_scatter(partial_out, "head", scatter_dimension=1, tiled=True)
    return gate_scale[None, :] * summed


def solution(mesh):
    def fused(queries, fresh_keys, fresh_values, stale_keys, stale_values, out_weight, gate_scale):
        summed = fused_sublayer(
            n_patch, n_head, queries, fresh_keys, fresh_values, stale_keys, stale_values, out_weight
        )
        return gate_scale[None, :] * summed.astype(jnp.float32)

    n_patch, n_head = mesh.shape["patch"], mesh.shape["head"]
    square = n_patch == n_head and n_head % CORES == 0
    return jax.shard_map(
        fused if square else on_device,
        mesh=mesh,
        in_specs=(
            P(("groups", "patch"), "head"),
            P(("groups", "patch"), "head"),
            P(("groups", "patch"), "head"),
            P(("groups", "patch"), "head"),
            P(("groups", "patch"), "head"),
            P("head", "patch"),
            P(("groups", "head")),
        ),
        out_specs=P(("groups", "patch"), "head"),
        check_vma=False,
    )
```

time: 65.5 us -> 73.5 us (1.12)
  Pallas kernels: 58.4 us -> 71.3 us
  local copies, waits for them, and re-layouts: 5.75 us -> 0.01 us
  other arithmetic: 1.01 us -> 2.04 us
    pallas_call x1, Pallas kernels: 58.4 us -> 71.3 us  [fused_sublayer(): pl.pallas_call(functools.partial(sublayer_kernel, n_patch, n_head), out_s...]
    unnamed x14 -> x2, local copies, waits for them, and re-layouts: 5.75 us -> 0.01 us
    mul x1, other arithmetic: 1.01 us -> 2.04 us  [fused(): return gate_scale[None, :] * summed.astype(jnp.float32)]
where the time goes in v2:
time: 73.5 us; the launch traced here: 73.4 us
  Pallas kernels  71.3 us (97%)
  other arithmetic  2.04 us (3%)
    pallas_call x1, Pallas kernels, fused_sublayer(): pl.pallas_call(functools.partial(sublayer_kernel, n_patch, n_head), out_s...  71.3 us
    mul x1, other arithmetic, fused(): return gate_scale[None, :] * summed.astype(jnp.float32)  2.04 us

profile of v2, /device:TPU:25, one launch (start us, length us, event | category | flops | bytes accessed | tf_op | source)
XLA Modules:
  0.0 73.4 jit_solution(15404963666408152280)
XLA Ops:
  0.0 0.0 copy-start
  0.0 71.3 %shard_map.73 = bf16[192,1280]{1,0:T(8,128)(2,1)} custom-call(bf16[192,384]{1,0:T(8,128)(2,1)} %q_hbm.1, bf16[192,384]{1,0:T(8,128)(2,1)} %fk_hbm.1, bf16[192,384]{1,0:T(8,128)(2,1)} %fv_hbm.1, bf16[192,384]{1,0:T(8,128)(2,1)} %sk_hbm.1, bf16[192,384]{1,0:T(8,128)(2,1)} %sv_hbm.1, bf16[384,1280]{1,0:T(8,128)(2,1)} %w_hbm.1), custom_call_target="tpu_custom_call" | custom-call | tf_op jit(solution)/shard_map/pallas_call | solution.py:347
  71.3 0.0 copy-done
  71.3 2.0 %convert_multiply_fusion = f32[192,1280]{1,0:T(8,128)} fusion(bf16[192,1280]{1,0:T(8,128)(2,1)} %shard_map.73, f32[1280]{0:T(1024)S(1)} %copy-done), kind=kLoop, calls=%fused_computation | loop fusion | flops 491520 | bytes 1479680 | tf_op jit(solution)/shard_map/mul | solution.py:427
Async XLA Ops:
  0.0 71.3 %copy-start = (f32[1280]{0:T(1024)S(1)}, f32[1280]{0:T(1024)}, u32[]{:S(2)}) copy-start(f32[1280]{0:T(1024)} %param.13) | copy-start | bytes 15364

commit v3 on v1

--- a/solution.py
+++ b/solution.py
@@ -50,9 +50,9 @@
 
 
 def sublayer_kernel(
-    n_patch, n_head, q_ref, fk_ref, fv_ref, sk_ref, sv_ref, w_ref, out_ref,
-    kbuf, vbuf, wsub, wbuf, abuf, ostage, obuf, top, total, acc,
-    kv_send, kv_recv, w_send, w_recv, z_send, x_send, sib_send, a_recv, o_send, o_recv,
+    n_patch, n_head, q_hbm, fk_hbm, fv_hbm, sk_hbm, sv_hbm, w_hbm, out_ref,
+    q_ref, fk_ref, fv_ref, w_ref, kbuf, vbuf, wsub, wbuf, abuf, ostage, obuf, top, total, acc,
+    load, kv_send, kv_recv, w_send, w_recv, z_send, x_send, sib_send, a_recv, o_send, o_recv,
 ):
     g, p, h = lax.axis_index("groups"), lax.axis_index("patch"), lax.axis_index("head")
     core, chip = lax.rem(h, CORES), lax.div(h, CORES)
@@ -67,9 +67,14 @@
             @pl.when(jnp.logical_or(p != s, h != j))
             def _():
                 pl.semaphore_signal(barrier, inc=1, device_id=(g, s, j), device_id_type=MESH)
-    for j in range(n_head):
-        wsub[j] = w_ref[:, j * sub:(j + 1) * sub]
-    wbuf[h] = wsub[h]
+    loads = [
+        pltpu.make_async_copy(src, dst, load.at[k])
+        for k, (src, dst) in enumerate(
+            ((w_hbm, w_ref), (q_hbm, q_ref), (fk_hbm, fk_ref), (fv_hbm, fv_ref))
+        )
+    ]
+    for copy in loads:
+        copy.start()
     pl.semaphore_wait(barrier, n_patch * n_head - 1)
 
     def remote(src, dst, send, recv, patch, head):
@@ -96,7 +101,7 @@
             src, buf.at[s], kv_send.at[side, which, s], kv_recv.at[which, s], neighbour(side), h
         )
 
-    for which, src in ((0, sk_ref), (1, sv_ref)):
+    for which, src in ((0, sk_hbm), (1, sv_hbm)):
         for side in range(2):
             @pl.when(has_neighbour(side))
             def _():
@@ -105,10 +110,16 @@
     def w_copy(j):
         return remote(wsub.at[j], wbuf.at[h], w_send.at[j], w_recv.at[h], p, j)
 
+    loads[0].wait()
     for j in range(n_head):
+        wsub[j] = w_ref[:, j * sub:(j + 1) * sub]
+
         @pl.when(h != j)
         def _():
             w_copy(j).start()
+    wbuf[h] = wsub[h]
+    for copy in loads[1:]:
+        copy.wait()
 
     def absorb_block(keys, values, first):
         for i in range(heads):
@@ -163,10 +174,11 @@
     for i in range(heads):
         abuf[p, h, :, i * HEAD_DIM:(i + 1) * HEAD_DIM] = (acc[i] / total[i]).astype(jnp.bfloat16)
 
-    def z_copy(side, s):
-        return remote(
-            abuf.at[s, h], abuf.at[s, h], z_send.at[side, s], a_recv.at[s, h], neighbour(side), h
-        )
+    def z_copy(s):
+        return remote(abuf.at[p, h], abuf.at[p, h], z_send.at[s], a_recv.at[p, h], s, h)
+
+    def z_arrival(s):
+        return remote(abuf.at[s, h], abuf.at[s, h], z_send.at[s], a_recv.at[s, h], s, h)
 
     def x_copy(xx, s):
         return remote(
@@ -185,11 +197,12 @@
                 x_copy(xx, s).start()
         sib_copy(s, h).start()
 
-    for side in range(2):
-        @pl.when(has_neighbour(side))
-        def _():
-            z_copy(side, p).start()
     spread(p)
+    for d in range(1, n_patch):
+        for side in range(2):
+            @pl.when(is_slab(side, d))
+            def _():
+                z_copy(slab_at(side, d)).start()
 
     for j in range(n_head):
         @pl.when(h != j)
@@ -228,12 +241,7 @@
 
             @pl.when(is_slab(side, d))
             def _():
-                copy = z_copy(side, s)
-                copy.wait_recv()
-
-                @pl.when(has_neighbour(side))
-                def _():
-                    copy.start()
+                z_arrival(s).wait_recv()
                 spread(s)
         for side in range(2):
             s = slab_at(side, d - 1)
@@ -278,7 +286,10 @@
             def _():
                 kv_copy(side, 0, s, kbuf.at[s]).wait_send()
                 kv_copy(side, 1, s, vbuf.at[s]).wait_send()
-                z_copy(side, s).wait_send()
+
+        @pl.when(s != p)
+        def _():
+            z_copy(s).wait_send()
         for xx in range(n_head // CORES):
             @pl.when(chip != xx)
             def _():
@@ -302,9 +313,13 @@
     return pl.pallas_call(
         functools.partial(sublayer_kernel, n_patch, n_head),
         out_shape=jax.ShapeDtypeStruct((rows, columns), bf16),
-        in_specs=[pl.BlockSpec(memory_space=pltpu.VMEM)] * 6,
+        in_specs=[pl.BlockSpec(memory_space=pl.ANY)] * 6,
         out_specs=pl.BlockSpec(memory_space=pltpu.VMEM),
         scratch_shapes=[
+            pltpu.VMEM((rows, width), bf16),
+            pltpu.VMEM((rows, width), bf16),
+            pltpu.VMEM((rows, width), bf16),
+            pltpu.VMEM((width, columns), bf16),
             pltpu.VMEM((n_patch, rows, width), bf16),
             pltpu.VMEM((n_patch, rows, width), bf16),
             pltpu.VMEM((n_head, width, sub), bf16),
@@ -315,11 +330,12 @@
             pltpu.VMEM((heads, rows, 1), jnp.float32),
             pltpu.VMEM((heads, rows, 1), jnp.float32),
             pltpu.VMEM((heads, rows, HEAD_DIM), jnp.float32),
+            dma((4,)),
             dma((2, 2, n_patch)),
             dma((2, n_patch)),
             dma((n_head,)),
             dma((n_head,)),
-            dma((2, n_patch)),
+            dma((n_patch,)),
             dma((n_head // CORES, n_patch)),
             dma((n_patch, n_head)),
             dma((n_patch, n_head)),
@@ -327,7 +343,7 @@
             dma((n_head,)),
         ],
         compiler_params=pltpu.CompilerParams(
-            collective_id=0, has_side_effects=True, vmem_limit_bytes=40 * 1024 * 1024
+            collective_id=0, has_side_effects=True, vmem_limit_bytes=56 * 1024 * 1024
         ),
     )(queries, fresh_keys, fresh_values, stale_keys, stale_values, out_weight)
 

time: 65.5 us -> 64.4 us (0.983)
  the two profiles are of different devices: /device:TPU:25 before, /device:TPU:2 now
where the time goes in v3:
time: 64.4 us; the launch traced here: 64.2 us
  Pallas kernels  62.2 us (97%)
  other arithmetic  2.04 us (3%)
    pallas_call x1, Pallas kernels, fused_sublayer(): pl.pallas_call(functools.partial(sublayer_kernel, n_patch, n_head), out_s...  62.2 us
    mul x1, other arithmetic, fused(): return gate_scale[None, :] * summed.astype(jnp.float32)  2.04 us

profile of v3, /device:TPU:2, one launch (start us, length us, event | category | flops | bytes accessed | tf_op | source)
XLA Modules:
  0.0 64.2 jit_solution(1551638930749779415)
XLA Ops:
  0.0 0.0 copy-start
  0.0 62.2 %shard_map.73 = bf16[192,1280]{1,0:T(8,128)(2,1)} custom-call(bf16[192,384]{1,0:T(8,128)(2,1)} %q_hbm.1, bf16[192,384]{1,0:T(8,128)(2,1)} %fk_hbm.1, bf16[192,384]{1,0:T(8,128)(2,1)} %fv_hbm.1, bf16[192,384]{1,0:T(8,128)(2,1)} %sk_hbm.1, bf16[192,384]{1,0:T(8,128)(2,1)} %sv_hbm.1, bf16[384,1280]{1,0:T(8,128)(2,1)} %w_hbm.1), custom_call_target="tpu_custom_call" | custom-call | tf_op jit(solution)/shard_map/pallas_call | solution.py:313
  62.2 0.0 copy-done
  62.2 2.0 %convert_multiply_fusion = f32[192,1280]{1,0:T(8,128)} fusion(bf16[192,1280]{1,0:T(8,128)(2,1)} %shard_map.73, f32[1280]{0:T(1024)S(1)} %copy-done), kind=kLoop, calls=%fused_computation | loop fusion | flops 491520 | bytes 1479680 | tf_op jit(solution)/shard_map/mul | solution.py:393
Async XLA Ops:
  0.0 62.2 %copy-start = (f32[1280]{0:T(1024)S(1)}, f32[1280]{0:T(1024)}, u32[]{:S(2)}) copy-start(f32[1280]{0:T(1024)} %param.13) | copy-start | bytes 15364

commit v4 on v2

--- a/solution.py
+++ b/solution.py
@@ -51,7 +51,7 @@
 
 def sublayer_kernel(
     n_patch, n_head, q_hbm, fk_hbm, fv_hbm, sk_hbm, sv_hbm, w_hbm, out_ref,
-    q_ref, fk_ref, fv_ref, w_ref,
+    q_ref, fk_ref, fv_ref, sk_ref, sv_ref, w_ref,
     kbuf, vbuf, wsub, wbuf, abuf, ostage, obuf, top, total, acc,
     load, kv_send, kv_recv, w_send, w_recv, z_send, x_send, sib_send, a_recv, o_send, o_recv,
 ):
@@ -72,14 +72,19 @@
             @pl.when(jnp.logical_or(p != s, h != j))
             def _():
                 pl.semaphore_signal(barrier, inc=1, device_id=(g, s, j), device_id_type=MESH)
+    pairs = [
+        (src.at[:, i * HEAD_DIM:(i + 1) * HEAD_DIM], dst.at[i])
+        for i in range(heads) for src, dst in ((sk_hbm, sk_ref), (sv_hbm, sv_ref))
+    ]
+    pairs += [(w_hbm, w_ref), (q_hbm, q_ref), (fk_hbm, fk_ref), (fv_hbm, fv_ref)]
     loads = [
-        pltpu.make_async_copy(src, dst, load.at[k])
-        for k, (src, dst) in enumerate(
-            ((w_hbm, w_ref), (q_hbm, q_ref), (fk_hbm, fk_ref), (fv_hbm, fv_ref))
-        )
+        pltpu.make_async_copy(src, dst, load.at[k]) for k, (src, dst) in enumerate(pairs)
     ]
     for copy in loads:
         copy.start()
+    for copy in loads[:2 * heads]:
+        copy.wait()
+    loads = loads[2 * heads:]
     pl.semaphore_wait(barrier, n_patch * n_head - 1)
 
     def remote(src, dst, send, recv, patch, head):
@@ -103,12 +108,12 @@
     def kv_copy(side, which, s, i, src):
         buf = (kbuf, vbuf)[which]
         return remote(
-            src.at[:, columns(i)], buf.at[s, :, columns(i)], kv_send.at[side, which, s, i],
+            src.at[i], buf.at[s, i], kv_send.at[side, which, s, i],
             kv_recv.at[which, s, i], neighbour(side), h,
         )
 
     def send_own(i):
-        for which, src in ((0, sk_hbm), (1, sv_hbm)):
+        for which, src in ((0, sk_ref), (1, sv_ref)):
             for side in range(2):
                 @pl.when(has_neighbour(side))
                 def _():
@@ -172,10 +177,10 @@
 
             @pl.when(is_slab(side, d))
             def _():
-                absorb_block(i, kbuf[s, :, columns(i)], vbuf[s, :, columns(i)], False)
+                absorb_block(i, kbuf[s, i], vbuf[s, i], False)
 
     def piece(s, head, i):
-        return abuf.at[s, head, :, columns(i)]
+        return abuf.at[s, head, i]
 
     def z_copy(side, s, i):
         return remote(
@@ -216,9 +221,10 @@
                     piece(s, head, i), piece(s, head, i), sib_send.at[s, h, i],
                     a_recv.at[s, head, i], p, sibling,
                 ).wait_recv()
-        term = jnp.dot(abuf[s, 0], wbuf[0], preferred_element_type=jnp.float32)
-        for j in range(1, n_head):
-            term = term + jnp.dot(abuf[s, j], wbuf[j], preferred_element_type=jnp.float32)
+        term = 0.0
+        for j in range(n_head):
+            group = jnp.concatenate([abuf[s, j, i] for i in range(heads)], axis=1)
+            term = term + jnp.dot(group, wbuf[j], preferred_element_type=jnp.float32)
         ostage[s] = term.astype(jnp.bfloat16)
 
         @pl.when(stays(s))
@@ -290,7 +296,7 @@
 
         @pl.when(i < heads)
         def _():
-            abuf[p, h, :, columns(i)] = (acc[...] / total[...]).astype(jnp.bfloat16)
+            abuf[p, h, i] = (acc[...] / total[...]).astype(jnp.bfloat16)
             for side in range(2):
                 @pl.when(has_neighbour(side))
                 def _():
@@ -353,18 +359,20 @@
             pltpu.VMEM((rows, width), bf16),
             pltpu.VMEM((rows, width), bf16),
             pltpu.VMEM((rows, width), bf16),
+            pltpu.VMEM((heads, rows, HEAD_DIM), bf16),
+            pltpu.VMEM((heads, rows, HEAD_DIM), bf16),
             pltpu.VMEM((width, columns), bf16),
-            pltpu.VMEM((n_patch, rows, width), bf16),
-            pltpu.VMEM((n_patch, rows, width), bf16),
+            pltpu.VMEM((n_patch, heads, rows, HEAD_DIM), bf16),
+            pltpu.VMEM((n_patch, heads, rows, HEAD_DIM), bf16),
             pltpu.VMEM((n_head, width, sub), bf16),
             pltpu.VMEM((n_head, width, sub), bf16),
-            pltpu.VMEM((n_patch, n_head, rows, width), bf16),
+            pltpu.VMEM((n_patch, n_head, heads, rows, HEAD_DIM), bf16),
             pltpu.VMEM((n_patch, rows, sub), bf16),
             pltpu.VMEM((n_head, rows, sub), bf16),
             pltpu.VMEM((rows, 1), jnp.float32),
             pltpu.VMEM((rows, 1), jnp.float32),
             pltpu.VMEM((rows, HEAD_DIM), jnp.float32),
-            dma((4,)),
+            dma((2 * heads + 4,)),
             dma((2, 2, n_patch, heads)),
             dma((2, n_patch, heads)),
             dma((n_head,)),

time: 73.5 us -> 73.4 us (level)
  no operation moved by 1% of the time
where the time goes in v4:
time: 73.4 us; the launch traced here: 73.2 us
  Pallas kernels  71.1 us (97%)
  other arithmetic  2.04 us (3%)
    pallas_call x1, Pallas kernels, fused_sublayer(): pl.pallas_call(functools.partial(sublayer_kernel, n_patch, n_head), out_s...  71.1 us
    mul x1, other arithmetic, fused(): return gate_scale[None, :] * summed.astype(jnp.float32)  2.04 us

profile of v4, /device:TPU:25, one launch (start us, length us, event | category | flops | bytes accessed | tf_op | source)
XLA Modules:
  0.0 73.2 jit_solution(11085132640742582356)
XLA Ops:
  0.0 0.0 copy-start
  0.0 71.1 %shard_map.73 = bf16[192,1280]{1,0:T(8,128)(2,1)} custom-call(bf16[192,384]{1,0:T(8,128)(2,1)} %q_hbm.1, bf16[192,384]{1,0:T(8,128)(2,1)} %fk_hbm.1, bf16[192,384]{1,0:T(8,128)(2,1)} %fv_hbm.1, bf16[192,384]{1,0:T(8,128)(2,1)} %sk_hbm.1, bf16[192,384]{1,0:T(8,128)(2,1)} %sv_hbm.1, bf16[384,1280]{1,0:T(8,128)(2,1)} %w_hbm.1), custom_call_target="tpu_custom_call" | custom-call | tf_op jit(solution)/shard_map/pallas_call | solution.py:353
  71.1 0.0 copy-done
  71.1 2.0 %convert_multiply_fusion = f32[192,1280]{1,0:T(8,128)} fusion(bf16[192,1280]{1,0:T(8,128)(2,1)} %shard_map.73, f32[1280]{0:T(1024)S(1)} %copy-done), kind=kLoop, calls=%fused_computation | loop fusion | flops 491520 | bytes 1479680 | tf_op jit(solution)/shard_map/mul | solution.py:435
Async XLA Ops:
  0.0 71.1 %copy-start = (f32[1280]{0:T(1024)S(1)}, f32[1280]{0:T(1024)}, u32[]{:S(2)}) copy-start(f32[1280]{0:T(1024)} %param.13) | copy-start | bytes 15364

commit v5 on v3

--- a/solution.py
+++ b/solution.py
@@ -174,11 +174,10 @@
     for i in range(heads):
         abuf[p, h, :, i * HEAD_DIM:(i + 1) * HEAD_DIM] = (acc[i] / total[i]).astype(jnp.bfloat16)
 
-    def z_copy(s):
-        return remote(abuf.at[p, h], abuf.at[p, h], z_send.at[s], a_recv.at[p, h], s, h)
-
-    def z_arrival(s):
-        return remote(abuf.at[s, h], abuf.at[s, h], z_send.at[s], a_recv.at[s, h], s, h)
+    def z_copy(side, s):
+        return remote(
+            abuf.at[s, h], abuf.at[s, h], z_send.at[side, s], a_recv.at[s, h], neighbour(side), h
+        )
 
     def x_copy(xx, s):
         return remote(
@@ -197,12 +196,11 @@
                 x_copy(xx, s).start()
         sib_copy(s, h).start()
 
+    for side in range(2):
+        @pl.when(has_neighbour(side))
+        def _():
+            z_copy(side, p).start()
     spread(p)
-    for d in range(1, n_patch):
-        for side in range(2):
-            @pl.when(is_slab(side, d))
-            def _():
-                z_copy(slab_at(side, d)).start()
 
     for j in range(n_head):
         @pl.when(h != j)
@@ -241,7 +239,12 @@
 
             @pl.when(is_slab(side, d))
             def _():
-                z_arrival(s).wait_recv()
+                copy = z_copy(side, s)
+                copy.wait_recv()
+
+                @pl.when(has_neighbour(side))
+                def _():
+                    copy.start()
                 spread(s)
         for side in range(2):
             s = slab_at(side, d - 1)
@@ -286,10 +289,7 @@
             def _():
                 kv_copy(side, 0, s, kbuf.at[s]).wait_send()
                 kv_copy(side, 1, s, vbuf.at[s]).wait_send()
-
-        @pl.when(s != p)
-        def _():
-            z_copy(s).wait_send()
+                z_copy(side, s).wait_send()
         for xx in range(n_head // CORES):
             @pl.when(chip != xx)
             def _():
@@ -335,7 +335,7 @@
             dma((2, n_patch)),
             dma((n_head,)),
             dma((n_head,)),
-            dma((n_patch,)),
+            dma((2, n_patch)),
             dma((n_head // CORES, n_patch)),
             dma((n_patch, n_head)),
             dma((n_patch, n_head)),

time: 64.4 us -> 61.7 us (0.958)
  the two profiles are of different devices: /device:TPU:2 before, /device:TPU:25 now
where the time goes in v5:
time: 61.7 us; the launch traced here: 61.6 us
  Pallas kernels  59.5 us (96%)
  other arithmetic  2.04 us (3%)
    pallas_call x1, Pallas kernels, fused_sublayer(): pl.pallas_call(functools.partial(sublayer_kernel, n_patch, n_head), out_s...  59.5 us
    mul x1, other arithmetic, fused(): return gate_scale[None, :] * summed.astype(jnp.float32)  2.04 us

profile of v5, /device:TPU:25, one launch (start us, length us, event | category | flops | bytes accessed | tf_op | source)
XLA Modules:
  0.0 61.6 jit_solution(466554519091029153)
XLA Ops:
  0.0 0.0 copy-start
  0.0 59.5 %shard_map.73 = bf16[192,1280]{1,0:T(8,128)(2,1)} custom-call(bf16[192,384]{1,0:T(8,128)(2,1)} %q_hbm.1, bf16[192,384]{1,0:T(8,128)(2,1)} %fk_hbm.1, bf16[192,384]{1,0:T(8,128)(2,1)} %fv_hbm.1, bf16[192,384]{1,0:T(8,128)(2,1)} %sk_hbm.1, bf16[192,384]{1,0:T(8,128)(2,1)} %sv_hbm.1, bf16[384,1280]{1,0:T(8,128)(2,1)} %w_hbm.1), custom_call_target="tpu_custom_call" | custom-call | tf_op jit(solution)/shard_map/pallas_call | solution.py:313
  59.5 0.0 copy-done
  59.5 2.0 %convert_multiply_fusion = f32[192,1280]{1,0:T(8,128)} fusion(bf16[192,1280]{1,0:T(8,128)(2,1)} %shard_map.73, f32[1280]{0:T(1024)S(1)} %copy-done), kind=kLoop, calls=%fused_computation | loop fusion | flops 491520 | bytes 1479680 | tf_op jit(solution)/shard_map/mul | solution.py:393
Async XLA Ops:
  0.0 59.5 %copy-start = (f32[1280]{0:T(1024)S(1)}, f32[1280]{0:T(1024)}, u32[]{:S(2)}) copy-start(f32[1280]{0:T(1024)} %param.13) | copy-start | bytes 15364

commit v6 on v5

--- a/solution.py
+++ b/solution.py
@@ -10,6 +10,7 @@
 HEAD_DIM = 128
 MESH = pl.DeviceIdType.MESH
 CORES = 2
+LANES = 128
 
 
 neg_large = -1e30
@@ -51,13 +52,22 @@
 
 def sublayer_kernel(
     n_patch, n_head, q_hbm, fk_hbm, fv_hbm, sk_hbm, sv_hbm, w_hbm, out_ref,
-    q_ref, fk_ref, fv_ref, w_ref, kbuf, vbuf, wsub, wbuf, abuf, ostage, obuf, top, total, acc,
+    q_ref, fk_ref, fv_ref, w_ref, kbuf, vbuf, wbuf, abuf, ostage, obuf, top, total, acc,
     load, kv_send, kv_recv, w_send, w_recv, z_send, x_send, sib_send, a_recv, o_send, o_recv,
 ):
     g, p, h = lax.axis_index("groups"), lax.axis_index("patch"), lax.axis_index("head")
     core, chip = lax.rem(h, CORES), lax.div(h, CORES)
     sibling = h + 1 - 2 * core
-    sub = wsub.shape[2]
+    pair = w_ref.shape[1] // (n_head // CORES)
+    wide = wbuf.shape[2]
+    starts = [j // CORES * pair + j % CORES * wide for j in range(n_head)]
+    widths = [wide if j % CORES == 0 else pair - wide for j in range(n_head)]
+
+    def on_core(action):
+        for c in range(CORES):
+            @pl.when(core == c)
+            def _():
+                action(widths[c])
     heads = q_ref.shape[1] // HEAD_DIM
     scale = HEAD_DIM ** (-0.5)
 
@@ -107,17 +117,23 @@
             def _():
                 kv_copy(side, which, p, src).start()
 
+    def w_part(j):
+        return w_ref.at[:, starts[j]:starts[j] + widths[j]]
+
     def w_copy(j):
-        return remote(wsub.at[j], wbuf.at[h], w_send.at[j], w_recv.at[h], p, j)
+        return remote(
+            w_part(j), wbuf.at[h, :, :widths[j]], w_send.at[j], w_recv.at[h], p, j
+        )
 
     loads[0].wait()
     for j in range(n_head):
-        wsub[j] = w_ref[:, j * sub:(j + 1) * sub]
-
         @pl.when(h != j)
         def _():
             w_copy(j).start()
-    wbuf[h] = wsub[h]
+
+        @pl.when(h == j)
+        def _():
+            wbuf[j, :, :widths[j]] = w_part(j)[...]
     for copy in loads[1:]:
         copy.wait()
 
@@ -205,10 +221,15 @@
     for j in range(n_head):
         @pl.when(h != j)
         def _():
-            remote(wsub.at[j], wbuf.at[j], w_send.at[j], w_recv.at[j], p, j).wait_recv()
-
-    def o_copy(s):
-        return remote(ostage.at[s], obuf.at[h], o_send.at[s], o_recv.at[h], s, p)
+            def arrived(width):
+                part = wbuf.at[j, :, :width]
+                remote(part, part, w_send.at[j], w_recv.at[j], p, j).wait_recv()
+            on_core(arrived)
+
+    def o_copy(s, width):
+        return remote(
+            ostage.at[s, :, :width], obuf.at[h, :, :width], o_send.at[s], o_recv.at[h], s, p
+        )
 
     def stays(s):
         return jnp.logical_and(s == p, h == p)
@@ -220,18 +241,23 @@
                 abuf.at[s, head], abuf.at[s, head], sib_send.at[s, h], a_recv.at[s, head], p, sibling
             )
             sib_in.wait_recv()
-        term = jnp.dot(abuf[s, 0], wbuf[0], preferred_element_type=jnp.float32)
-        for j in range(1, n_head):
-            term = term + jnp.dot(abuf[s, j], wbuf[j], preferred_element_type=jnp.float32)
-        ostage[s] = term.astype(jnp.bfloat16)
-
-        @pl.when(stays(s))
-        def _():
-            obuf[h] = ostage[s]
-
-        @pl.when(jnp.logical_not(stays(s)))
-        def _():
-            o_copy(s).start()
+        def finish(width):
+            term = jnp.dot(abuf[s, 0], wbuf[0, :, :width], preferred_element_type=jnp.float32)
+            for j in range(1, n_head):
+                term = term + jnp.dot(
+                    abuf[s, j], wbuf[j, :, :width], preferred_element_type=jnp.float32
+                )
+            ostage[s, :, :width] = term.astype(jnp.bfloat16)
+
+            @pl.when(stays(s))
+            def _():
+                obuf[h, :, :width] = ostage[s, :, :width]
+
+            @pl.when(jnp.logical_not(stays(s)))
+            def _():
+                o_copy(s, width).start()
+
+        on_core(finish)
 
     def spread_step(d, carry):
         for side in range(2):
@@ -273,8 +299,9 @@
     for j in range(n_head):
         @pl.when(jnp.logical_or(p != h, h != j))
         def _():
-            remote(ostage.at[0], obuf.at[j], o_send.at[0], o_recv.at[j], h, j).wait_recv()
-        out_ref[:, j * sub:(j + 1) * sub] = obuf[j]
+            part = obuf.at[j, :, :widths[j]]
+            remote(part, part, o_send.at[0], o_recv.at[j], h, j).wait_recv()
+        out_ref[:, starts[j]:starts[j] + widths[j]] = obuf[j, :, :widths[j]]
 
     for j in range(n_head):
         @pl.when(h != j)
@@ -298,7 +325,7 @@
 
         @pl.when(jnp.logical_not(stays(s)))
         def _():
-            o_copy(s).wait_send()
+            on_core(lambda width: o_copy(s, width).wait_send())
         return carry
 
     lax.fori_loop(0, n_patch, drain, 0)
@@ -307,7 +334,7 @@
 def fused_sublayer(n_patch, n_head, queries, fresh_keys, fresh_values, stale_keys, stale_values, out_weight):
     rows, width = queries.shape
     columns = out_weight.shape[1]
-    sub = columns // n_head
+    sub = -(-(columns // (n_head // CORES)) // (2 * LANES)) * LANES
     heads = width // HEAD_DIM
     bf16, dma = jnp.bfloat16, pltpu.SemaphoreType.DMA
     return pl.pallas_call(
@@ -322,7 +349,6 @@
             pltpu.VMEM((width, columns), bf16),
             pltpu.VMEM((n_patch, rows, width), bf16),
             pltpu.VMEM((n_patch, rows, width), bf16),
-            pltpu.VMEM((n_head, width, sub), bf16),
             pltpu.VMEM((n_head, width, sub), bf16),
             pltpu.VMEM((n_patch, n_head, rows, width), bf16),
             pltpu.VMEM((n_patch, rows, sub), bf16),

time: 61.7 us -> 59 us (0.956)
  Pallas kernels: 59.5 us -> 56.8 us
    pallas_call x1, Pallas kernels: 59.5 us -> 56.8 us  [fused_sublayer(): pl.pallas_call(functools.partial(sublayer_kernel, n_patch, n_head), out_s...]
where the time goes in v6:
time: 59 us; the launch traced here: 58.9 us
  Pallas kernels  56.8 us (96%)
  other arithmetic  2.04 us (3%)
    pallas_call x1, Pallas kernels, fused_sublayer(): pl.pallas_call(functools.partial(sublayer_kernel, n_patch, n_head), out_s...  56.8 us
    mul x1, other arithmetic, fused(): return gate_scale[None, :] * summed.astype(jnp.float32)  2.04 us

profile of v6, /device:TPU:25, one launch (start us, length us, event | category | flops | bytes accessed | tf_op | source)
XLA Modules:
  0.0 58.9 jit_solution(4360053838816183322)
XLA Ops:
  0.0 0.0 copy-start
  0.0 56.8 %shard_map.73 = bf16[192,1280]{1,0:T(8,128)(2,1)} custom-call(bf16[192,384]{1,0:T(8,128)(2,1)} %q_hbm.1, bf16[192,384]{1,0:T(8,128)(2,1)} %fk_hbm.1, bf16[192,384]{1,0:T(8,128)(2,1)} %fv_hbm.1, bf16[192,384]{1,0:T(8,128)(2,1)} %sk_hbm.1, bf16[192,384]{1,0:T(8,128)(2,1)} %sv_hbm.1, bf16[384,1280]{1,0:T(8,128)(2,1)} %w_hbm.1), custom_call_target="tpu_custom_call" | custom-call | tf_op jit(solution)/shard_map/pallas_call | solution.py:340
  56.8 0.0 copy-done
  56.8 2.0 %convert_multiply_fusion = f32[192,1280]{1,0:T(8,128)} fusion(bf16[192,1280]{1,0:T(8,128)(2,1)} %shard_map.73, f32[1280]{0:T(1024)S(1)} %copy-done), kind=kLoop, calls=%fused_computation | loop fusion | flops 491520 | bytes 1479680 | tf_op jit(solution)/shard_map/mul | solution.py:419
Async XLA Ops:
  0.0 56.8 %copy-start = (f32[1280]{0:T(1024)S(1)}, f32[1280]{0:T(1024)}, u32[]{:S(2)}) copy-start(f32[1280]{0:T(1024)} %param.13) | copy-start | bytes 15364

commit v7 on v6

--- a/solution.py
+++ b/solution.py
@@ -52,13 +52,13 @@
 
 def sublayer_kernel(
     n_patch, n_head, q_hbm, fk_hbm, fv_hbm, sk_hbm, sv_hbm, w_hbm, out_ref,
-    q_ref, fk_ref, fv_ref, w_ref, kbuf, vbuf, wbuf, abuf, ostage, obuf, top, total, acc,
+    q_ref, fk_ref, fv_ref, kbuf, vbuf, wbuf, abuf, ostage, obuf, top, total, acc,
     load, kv_send, kv_recv, w_send, w_recv, z_send, x_send, sib_send, a_recv, o_send, o_recv,
 ):
     g, p, h = lax.axis_index("groups"), lax.axis_index("patch"), lax.axis_index("head")
     core, chip = lax.rem(h, CORES), lax.div(h, CORES)
     sibling = h + 1 - 2 * core
-    pair = w_ref.shape[1] // (n_head // CORES)
+    pair = w_hbm.shape[1] // (n_head // CORES)
     wide = wbuf.shape[2]
     starts = [j // CORES * pair + j % CORES * wide for j in range(n_head)]
     widths = [wide if j % CORES == 0 else pair - wide for j in range(n_head)]
@@ -80,7 +80,7 @@
     loads = [
         pltpu.make_async_copy(src, dst, load.at[k])
         for k, (src, dst) in enumerate(
-            ((w_hbm, w_ref), (q_hbm, q_ref), (fk_hbm, fk_ref), (fv_hbm, fv_ref))
+            ((q_hbm, q_ref), (fk_hbm, fk_ref), (fv_hbm, fv_ref))
         )
     ]
     for copy in loads:
@@ -118,14 +118,16 @@
                 kv_copy(side, which, p, src).start()
 
     def w_part(j):
-        return w_ref.at[:, starts[j]:starts[j] + widths[j]]
+        return w_hbm.at[:, starts[j]:starts[j] + widths[j]]
+
+    def w_own(j):
+        return pltpu.make_async_copy(w_part(j), wbuf.at[j, :, :widths[j]], w_send.at[j])
 
     def w_copy(j):
         return remote(
             w_part(j), wbuf.at[h, :, :widths[j]], w_send.at[j], w_recv.at[h], p, j
         )
 
-    loads[0].wait()
     for j in range(n_head):
         @pl.when(h != j)
         def _():
@@ -133,8 +135,8 @@
 
         @pl.when(h == j)
         def _():
-            wbuf[j, :, :widths[j]] = w_part(j)[...]
-    for copy in loads[1:]:
+            w_own(j).start()
+    for copy in loads:
         copy.wait()
 
     def absorb_block(keys, values, first):
@@ -226,6 +228,10 @@
                 remote(part, part, w_send.at[j], w_recv.at[j], p, j).wait_recv()
             on_core(arrived)
 
+        @pl.when(h == j)
+        def _():
+            w_own(j).wait()
+
     def o_copy(s, width):
         return remote(
             ostage.at[s, :, :width], obuf.at[h, :, :width], o_send.at[s], o_recv.at[h], s, p
@@ -346,7 +352,6 @@
             pltpu.VMEM((rows, width), bf16),
             pltpu.VMEM((rows, width), bf16),
             pltpu.VMEM((rows, width), bf16),
-            pltpu.VMEM((width, columns), bf16),
             pltpu.VMEM((n_patch, rows, width), bf16),
             pltpu.VMEM((n_patch, rows, width), bf16),
             pltpu.VMEM((n_head, width, sub), bf16),
@@ -356,7 +361,7 @@
             pltpu.VMEM((heads, rows, 1), jnp.float32),
             pltpu.VMEM((heads, rows, 1), jnp.float32),
             pltpu.VMEM((heads, rows, HEAD_DIM), jnp.float32),
-            dma((4,)),
+            dma((3,)),
             dma((2, 2, n_patch)),
             dma((2, n_patch)),
             dma((n_head,)),

time: 59 us -> 59 us (level)
  no operation moved by 1% of the time
where the time goes in v7:
time: 59 us; the launch traced here: 58.9 us
  Pallas kernels  56.8 us (96%)
  other arithmetic  2.04 us (3%)
    pallas_call x1, Pallas kernels, fused_sublayer(): pl.pallas_call(functools.partial(sublayer_kernel, n_patch, n_head), out_s...  56.8 us
    mul x1, other arithmetic, fused(): return gate_scale[None, :] * summed.astype(jnp.float32)  2.04 us

profile of v7, /device:TPU:25, one launch (start us, length us, event | category | flops | bytes accessed | tf_op | source)
XLA Modules:
  0.0 58.9 jit_solution(14170218653994022166)
XLA Ops:
  0.0 0.0 copy-start
  0.0 56.8 %shard_map.73 = bf16[192,1280]{1,0:T(8,128)(2,1)} custom-call(bf16[192,384]{1,0:T(8,128)(2,1)} %q_hbm.1, bf16[192,384]{1,0:T(8,128)(2,1)} %fk_hbm.1, bf16[192,384]{1,0:T(8,128)(2,1)} %fv_hbm.1, bf16[192,384]{1,0:T(8,128)(2,1)} %sk_hbm.1, bf16[192,384]{1,0:T(8,128)(2,1)} %sv_hbm.1, bf16[384,1280]{1,0:T(8,128)(2,1)} %w_hbm.1), custom_call_target="tpu_custom_call" | custom-call | tf_op jit(solution)/shard_map/pallas_call | solution.py:346
  56.8 0.0 copy-done
  56.8 2.0 %convert_multiply_fusion = f32[192,1280]{1,0:T(8,128)} fusion(bf16[192,1280]{1,0:T(8,128)(2,1)} %shard_map.73, f32[1280]{0:T(1024)S(1)} %copy-done), kind=kLoop, calls=%fused_computation | loop fusion | flops 491520 | bytes 1479680 | tf_op jit(solution)/shard_map/mul | solution.py:424
Async XLA Ops:
  0.0 56.8 %copy-start = (f32[1280]{0:T(1024)S(1)}, f32[1280]{0:T(1024)}, u32[]{:S(2)}) copy-start(f32[1280]{0:T(1024)} %param.13) | copy-start | bytes 15364
